TPU v7x, 32 devices: a whole 2x2x4 slice. The times are simulated.
32 devices in a mesh: pool: 1, fsdp: 32 (over z, y, x, core).
Axes of the slice: x: 2, y: 2, z: 4, core: 2. Of those that a mesh axis runs over, the one named last changes fastest.
Arguments:
- noisy: bfloat16 [2048, 2560], P(('pool', 'fsdp')), may hold values from -6 to 6
- clean: bfloat16 [2048, 2560], P(('pool', 'fsdp')), may hold values from -6 to 6
- seg_ids: int32 [32], P('pool'), may hold values from 0 to 3, never falling along the last dimension, each value on 1 to 12 neighbouring positions
- lag_mask: int32 [32, 2], P(('pool', 'fsdp')), may hold values 0 or 1
- plan: int32 [32, 2], P(('pool', 'fsdp')), may hold values from 1 to 999, as said below
- w_query: bfloat16 [2560, 2560], P('fsdp'), may hold values from -0.125 to 0.125
- w_key: bfloat16 [2560, 2560], P('fsdp'), may hold values from -0.125 to 0.125
- time_proj: bfloat16 [128, 7680], replicated, may hold values from -0.5 to 0.5
- q_gain: float32 [2560], replicated, may hold values from 0.5 to 14
- k_gain: float32 [2560], replicated, may hold values from 0.5 to 14
Outputs:
- denoised: bfloat16 [2048, 2560], P(('pool', 'fsdp'))
Inputs may be any that keep to these rules, and one draw needn't show every extreme that they name: seg_ids never falls along the spans; each rollout is 1 to 12 consecutive spans. `plan`: entry j of a row lies from 1000 * (1 - j) // 2 + 1 to 1000 * (2 - j) // 2 - 1, so each row falls strictly.
All inputs are finite; a program needn't handle non-finite values. No bound on the sum of `lag_mask` on one device may be relied on, other than what follows from the above.
Results may differ from a plain program's by a relative error of at most 0.024.
Values may be sent and summed in bfloat16 or wider, within the bound.
A program may use at most 128 MiB of HBM per device.

v0:
```python
import math

import jax
import jax.numpy as jnp
from jax import lax
from jax.sharding import PartitionSpec as P

HEADS = 20
HEAD_DIM = 128
STEPS = 2
LAGS = 2
LEVELS = 1000


SIGMA_SHIFT = 5.0
EPSILON = 1e-06
MASKED = -1e30


def passed_along(value, axis, steps):
    count = lax.axis_size(axis)
    leading, last = (max(0, -steps), min(count, count - steps))
    return lax.ppermute(value, axis, [(source, source + steps) for source in range(leading, last)])


def sigma_of(levels):
    fraction = levels.astype(jnp.float32) / LEVELS
    return SIGMA_SHIFT * fraction / (1.0 + (SIGMA_SHIFT - 1.0) * fraction)


def frequencies(half_count):
    return jnp.exp(-math.log(10000.0) * jnp.arange(half_count, dtype=jnp.float32) / half_count)


def modulation(sigmas, time_proj):
    half_count = time_proj.shape[0] // 2
    angles = 1000.0 * sigmas[:, None] * frequencies(half_count)[None, :]
    features = jnp.concatenate([jnp.cos(angles), jnp.sin(angles)], axis=1).astype(jnp.bfloat16)
    return jnp.dot(features, time_proj, preferred_element_type=jnp.float32)[0]


def modulate(latent, mod_row, model_width):
    values = latent.astype(jnp.float32)
    centred = values - jnp.mean(values, axis=-1, keepdims=True)
    variance = jnp.mean(centred * centred, axis=-1, keepdims=True)
    normed = centred * lax.rsqrt(variance + EPSILON)
    return (normed * (1.0 + mod_row[model_width : 2 * model_width]) + mod_row[:model_width]).astype(
        jnp.bfloat16
    )


def normalize(values, gain):
    mean_square = jnp.mean(values * values, axis=-1, keepdims=True)
    return values * lax.rsqrt(mean_square + EPSILON) * gain


def rotate(values, positions):
    half_count = HEAD_DIM // 2
    split_heads = values.reshape(values.shape[:-1] + (HEADS, HEAD_DIM))
    angles = positions[..., None] * frequencies(half_count)
    cosine = jnp.cos(angles)[..., None, :]
    sine = jnp.sin(angles)[..., None, :]
    front = split_heads[..., :half_count]
    back = split_heads[..., half_count:]
    turned = jnp.concatenate([front * cosine - back * sine, front * sine + back * cosine], axis=-1)
    return turned.reshape(values.shape)


def attend(query_rows, key_rows, value_rows, usable):
    row_count = query_rows.shape[0]
    query_heads = query_rows.reshape(row_count, HEADS, HEAD_DIM)
    key_heads = key_rows.reshape(-1, HEADS, HEAD_DIM)
    value_heads = value_rows.reshape(-1, HEADS, HEAD_DIM)
    scores = jnp.einsum(
        "qhd,khd->hqk", query_heads, key_heads, preferred_element_type=jnp.float32
    ) * HEAD_DIM ** (-0.5)
    scores = jnp.where(usable[None, None, :], scores, MASKED)
    highest = jnp.max(scores, axis=-1, keepdims=True)
    expanded = jnp.exp(scores - highest)
    weights = (expanded / jnp.sum(expanded, axis=-1, keepdims=True)).astype(jnp.bfloat16)
    mixed = jnp.einsum("hqk,khd->qhd", weights, value_heads, preferred_element_type=jnp.float32)
    return mixed.reshape(row_count, HEADS * HEAD_DIM).astype(jnp.bfloat16)


def make_absorbers(noisy_hidden, context_hidden):

    def absorb_both(carry, pieces, offset):
        stored = tuple((piece_rows for piece_rows in pieces))
        query_sum = jnp.dot(noisy_hidden, pieces[0], preferred_element_type=jnp.float32)
        key_sum = jnp.dot(noisy_hidden, pieces[1], preferred_element_type=jnp.float32)
        ctxkey_sum = jnp.dot(context_hidden, pieces[1], preferred_element_type=jnp.float32)
        return (stored, (query_sum, key_sum, ctxkey_sum))

    def absorb_key(carry, piece, offset):
        buffer_rows, partials = carry
        stored = lax.dynamic_update_slice_in_dim(buffer_rows, piece, offset, 0)
        key_sum, ctxkey_sum = partials
        key_sum = key_sum + jnp.dot(noisy_hidden, piece, preferred_element_type=jnp.float32)
        ctxkey_sum = ctxkey_sum + jnp.dot(context_hidden, piece, preferred_element_type=jnp.float32)
        return (stored, (key_sum, ctxkey_sum))

    def absorb_query(carry, piece, offset):
        buffer_rows, query_sum = carry
        stored = lax.dynamic_update_slice_in_dim(buffer_rows, piece, offset, 0)
        query_sum = query_sum + jnp.dot(noisy_hidden, piece, preferred_element_type=jnp.float32)
        return (stored, query_sum)

    return (absorb_both, absorb_key, absorb_query)


def local(noisy, clean, seg_ids, lag_mask, plan, w_query, w_key, time_proj, q_gain, k_gain):
    row_count, model_width = noisy.shape
    inner_width = w_query.shape[1]
    span_index = lax.axis_index("fsdp")
    segment_start = jnp.sum((seg_ids < seg_ids[span_index]).astype(jnp.int32))
    span_place = span_index - segment_start
    positions = (span_place * row_count + jnp.arange(row_count, dtype=jnp.int32)).astype(
        jnp.float32
    )
    sigmas = [sigma_of(plan[0, level_index : level_index + 1]) for level_index in range(STEPS)] + [
        jnp.zeros((1,), jnp.float32)
    ]
    rest_mod = modulation(jnp.zeros((1,), jnp.float32), time_proj)
    step_mods = [modulation(sigmas[level_index], time_proj) for level_index in range(STEPS)]
    context_hidden = modulate(clean, rest_mod, model_width)
    noisy_hidden = modulate(noisy, step_mods[0], model_width)
    absorb_both, absorb_key, absorb_query = make_absorbers(noisy_hidden, context_hidden)
    empty_buffer = jnp.zeros((model_width, inner_width), jnp.bfloat16)
    empty_sum = jnp.zeros((row_count, inner_width), jnp.float32)
    buffers, partials = absorb_both(
        ((empty_buffer, empty_buffer), (empty_sum, empty_sum, empty_sum)),
        (
            lax.all_gather(w_query, "fsdp", axis=0, tiled=True),
            lax.all_gather(w_key, "fsdp", axis=0, tiled=True),
        ),
        jnp.int32(0),
    )
    full_query, full_key = buffers
    query_sum, key_sum, ctxkey_sum = partials
    context_key = rotate(normalize(ctxkey_sum, k_gain), positions).astype(jnp.bfloat16)
    context_pair = jnp.stack([context_key, context_hidden])
    received = [passed_along(context_pair, "fsdp", 1)]
    distance = 2
    received.append(passed_along(context_pair, "fsdp", distance))
    usable_parts = [jnp.ones((row_count,), jnp.int32) > 0]
    for distance in range(1, LAGS + 1):
        source = jnp.maximum(span_index - distance, 0)
        allowed = (
            (span_index >= distance)
            & (seg_ids[source] == seg_ids[span_index])
            & (lag_mask[0, distance - 1] == 1)
        )
        usable_parts.append(jnp.broadcast_to(allowed, (row_count,)))
    usable = jnp.concatenate(usable_parts)
    keys_context = jnp.concatenate([pair_rows[0] for pair_rows in received], axis=0)
    values_context = jnp.concatenate([pair_rows[1] for pair_rows in received], axis=0)
    latent = noisy
    for step_index in range(STEPS):
        if step_index == 0:
            hidden = noisy_hidden
            query_raw, key_raw = (query_sum, key_sum)
        else:
            hidden = modulate(latent, step_mods[step_index], model_width)
            query_raw = jnp.dot(hidden, full_query, preferred_element_type=jnp.float32)
            key_raw = jnp.dot(hidden, full_key, preferred_element_type=jnp.float32)
        query_rows = rotate(normalize(query_raw, q_gain), positions).astype(jnp.bfloat16)
        key_rows = rotate(normalize(key_raw, k_gain), positions).astype(jnp.bfloat16)
        mixed = attend(
            query_rows,
            jnp.concatenate([key_rows, keys_context], axis=0),
            jnp.concatenate([hidden, values_context], axis=0),
            usable,
        )
        sigma_change = sigmas[step_index + 1] - sigmas[step_index]
        factor = sigma_change * step_mods[step_index][2 * model_width :]
        latent = (latent.astype(jnp.float32) + factor[None, :] * mixed.astype(jnp.float32)).astype(
            jnp.bfloat16
        )
    return latent


def solution(mesh):
    placed = (
        P(("pool", "fsdp"), None),
        P(("pool", "fsdp"), None),
        P("pool"),
        P(("pool", "fsdp"), None),
        P(("pool", "fsdp"), None),
        P("fsdp", None),
        P("fsdp", None),
        P(),
        P(),
        P(),
    )
    return jax.shard_map(
        local, mesh=mesh, in_specs=placed, out_specs=P(("pool", "fsdp"), None), check_vma=False
    )
```

profile of v0, /device:TPU:0, one launch (start us, length us, event | category | flops | bytes accessed | tf_op | source)
XLA Modules:
  0.0 296.4 jit_solution(1294598367972171601)
XLA Ops:
  8.0 1.3 fusion.99
  10.8 1.4 fusion.101
  12.2 2.0 fusion.50
  17.5 1.4 fusion.100
  21.0 1.1 convert_reduce_fusion.1
  22.2 1.1 convert_reduce_fusion.2
  23.3 1.2 fusion.30
  26.0 1.0 fusion.78
  26.9 84.5 %all-gather.3.cloned.1.call-done = bf16[2560,2560]{1,0:T(8,128)(2,1)} async-done(((bf16[80,2560]{1,0:T(8,128)(2,1)}), bf16[2560,2560]{1,0:T(8,128)(2,1)}) %all-gather.3.cloned.1.call-update) | async-done | bytes 13107216 | tf_op jit(solution)/shard_map/all_gather | solution.py:134
  111.4 7.4 %multiply_reduce_fusion.2 = (f32[64]{0:T(128)S(1)}, f32[64,2560]{1,0:T(8,128)S(1)}) fusion(bf16[2560,2560]{1,0:T(8,128)(2,1)} %all-gather.3.cloned.1.call-done, bf16[64,2560]{1,0:T(8,128)(2,1)S(1)} %copy-done.2, f32[2560]{0:T(1024)S(1)} %get-tuple-element.41, f32[2560]{0:T(1024)S(1)} %get-tuple-element.42, f32[64]{0:T(128)S(1)} %add_rsqrt_fusion.7, ...), kind=kOutput, calls=%fused_computation.79 | convolution fusion | flops 840171456 | bytes 14111488 | tf_op jit(solution)/shard_map/dot_general | solution.py:90
  118.9 1.0 copy-done.1
  119.9 2.5 multiply_reduce_fusion.4
  122.5 1.0 multiply_multiply_fusion.2
  123.4 1.0 reshape.305
  124.4 1.2 reshape.303
  125.6 2.8 fusion.95
  128.4 1.4 fusion.96
  129.8 81.3 %all-gather.5.cloned.1.call-done = bf16[2560,2560]{1,0:T(8,128)(2,1)} async-done(((bf16[80,2560]{1,0:T(8,128)(2,1)}), bf16[2560,2560]{1,0:T(8,128)(2,1)}) %all-gather.5.cloned.1.call-update) | async-done | bytes 13107216 | tf_op jit(solution)/shard_map/all_gather | solution.py:133
  211.1 7.3 %multiply_reduce_fusion.3 = (f32[64]{0:T(128)S(1)}, f32[64,2560]{1,0:T(8,128)S(1)}) fusion(bf16[2560,2560]{1,0:T(8,128)(2,1)} %all-gather.5.cloned.1.call-done, bf16[64,2560]{1,0:T(8,128)(2,1)S(1)} %copy-done.2, f32[2560]{0:T(1024)S(1)} %get-tuple-element.41, f32[2560]{0:T(1024)S(1)} %get-tuple-element.42, f32[64]{0:T(128)S(1)} %add_rsqrt_fusion.7, ...), kind=kOutput, calls=%fused_computation.83 | convolution fusion | flops 840171456 | bytes 14111488 | tf_op jit(solution)/shard_map/dot_general | solution.py:89
  218.4 1.0 multiply_multiply_fusion.3
  219.4 1.2 reshape.304
  220.9 0.8 copy-done.4
  222.4 1.8 subtract_convert_fusion.3
  225.2 0.9 pad_maximum_fusion.12
  226.1 2.2 collective-permute-start
  228.7 1.0 copy_bitcast_fusion.1
  229.7 4.1 %collective-permute-start.1 = (bf16[2,64,2560]{2,1,0:T(8,128)(2,1)}, bf16[2,64,2560]{2,1,0:T(8,128)(2,1)}, u32[]{:S(2)}, u32[]{:S(2)}) collective-permute-start(bf16[2,64,2560]{2,1,0:T(8,128)(2,1)} %pad_maximum_fusion.12), channel_id=1, source_target_pairs={{0,2},{1,3},{2,4},{3,5},{4,6},{5,7},{6,8},{7,9},{8,10},{9,11},{10,... | collective-permute-start | bytes 1966088 | tf_op jit(solution)/shard_map/ppermute | solution.py:23
  234.1 0.8 copy.31
  234.9 13.6 %collective-permute-done.1 = bf16[2,64,2560]{2,1,0:T(8,128)(2,1)} collective-permute-done((bf16[2,64,2560]{2,1,0:T(8,128)(2,1)}, bf16[2,64,2560]{2,1,0:T(8,128)(2,1)}, u32[]{:S(2)}, u32[]{:S(2)}) %collective-permute-start.1) | collective-permute-done | bytes 655392 | tf_op jit(solution)/shard_map/ppermute | solution.py:23
  248.5 1.8 fusion.98
  250.3 1.2 concatenate.89
  251.5 0.8 copy.32
  252.5 0.8 copy.25
  253.7 3.5 %fusion.102 = (f32[20,64]{1,0:T(8,128)S(1)}, f32[20,64,192]{2,1,0:T(8,128)}) fusion(bf16[64,20,128]{2,0,1:T(8,128)(2,1)} %copy.32, bf16[64,20,128]{2,0,1:T(8,128)(2,1)} %copy.31, bf16[64,20,64]{2,0,1:T(8,128)(2,1)} %get-tuple-element.33, bf16[64,20,64]{2,0,1:T(8,128)(2,1)} %get-tuple-element.34, pred[192]{0:T(512)(128)(4,1)S(1)} %copy-done.16, ...), kind=kOutput, calls=%fused_computation.168 | convolution fusion | flops 68485312 | bytes 2299072 | tf_op jit(solution)/shard_map/sub | solution.py:79
  257.2 1.9 fusion.11
  259.5 1.0 copy_bitcast_fusion
  260.5 7.3 %multiply_reduce_fusion = (f32[64]{0:T(128)S(1)}, f32[64,2560]{1,0:T(8,128)S(1)}) fusion(bf16[2560,2560]{1,0:T(8,128)(2,1)} %all-gather.3.cloned.1.call-done, bf16[64,2560]{1,0:T(8,128)(2,1)S(1)} %get-tuple-element.6, f32[2560]{0:T(1024)S(1)} %get-tuple-element.38, f32[2560]{0:T(1024)S(1)} %get-tuple-element.39, f32[64]{0:T(128)S(1)} %add_rsqrt_fusion.2, ...), kind=kOutput, calls=%fused_computation.71 | convolution fusion | flops 840171456 | bytes 14111488 | tf_op jit(solution)/shard_map/dot_general | solution.py:165
  267.8 1.0 multiply_multiply_fusion
  268.9 1.2 reshape.307
  270.0 1.4 fusion.93
  271.4 7.3 %multiply_reduce_fusion.1 = (f32[64]{0:T(128)S(1)}, f32[64,2560]{1,0:T(8,128)S(1)}) fusion(bf16[2560,2560]{1,0:T(8,128)(2,1)} %all-gather.5.cloned.1.call-done, bf16[64,2560]{1,0:T(8,128)(2,1)S(1)} %get-tuple-element.6, f32[2560]{0:T(1024)S(1)} %get-tuple-element.38, f32[2560]{0:T(1024)S(1)} %get-tuple-element.39, f32[64]{0:T(128)S(1)} %add_rsqrt_fusion.2, ...), kind=kOutput, calls=%fused_computation.75 | convolution fusion | flops 840171456 | bytes 14111488 | tf_op jit(solution)/shard_map/dot_general | solution.py:164
  278.7 1.0 multiply_multiply_fusion.1
  279.7 1.2 reshape.306
  281.2 0.8 copy-done.8
  282.3 1.2 subtract_convert_fusion.1
  283.5 3.2 %fusion.105 = (f32[20,64]{1,0:T(8,128)S(1)}, f32[20,64,192]{2,1,0:T(8,128)}) fusion(bf16[64,20,128]{2,0,1:T(8,128)(2,1)} %copy.32, bf16[64,20,128]{2,0,1:T(8,128)(2,1)} %copy.31, bf16[64,20,64]{2,0,1:T(8,128)(2,1)S(1)} %get-tuple-element.31, bf16[64,20,64]{2,0,1:T(8,128)(2,1)} %get-tuple-element.32, pred[192]{0:T(512)(128)(4,1)S(1)} %copy-done.16, ...), kind=kOutput, calls=%fused_computation.169 | convolution fusion | flops 68485312 | bytes 2299072 | tf_op jit(solution)/shard_map/sub | solution.py:79
  286.7 2.1 fusion.9
  288.8 0.8 fusion.39
  (76 shorter events, 7.8 us)
Async XLA Ops:
  6.5 18.3 %copy-start = (bf16[128,7680]{1,0:T(8,128)(2,1)S(1)}, bf16[128,7680]{1,0:T(8,128)(2,1)}, u32[]{:S(2)}) copy-start(bf16[128,7680]{1,0:T(8,128)(2,1)} %param.17) | copy-start | bytes 5898244
  6.5 18.0 %copy-start.3 = (bf16[64,2560]{1,0:T(8,128)(2,1)S(1)}, bf16[64,2560]{1,0:T(8,128)(2,1)}, u32[]{:S(2)}) copy-start(bf16[64,2560]{1,0:T(8,128)(2,1)} %param.11) | copy-start | bytes 983044
  6.5 104.9 %all-gather.3.cloned.1.call-start = ((), (), s32[]{:S(2)}) async-start(), calls=%async_computation | async-start | bytes 13516800 | tf_op jit(solution)/shard_map/all_gather | solution.py:134
  7.3 203.8 %all-gather.5.cloned.1.call-start = ((), (), s32[]{:S(2)}) async-start(), calls=%async_computation.1 | async-start | bytes 13516800 | tf_op jit(solution)/shard_map/all_gather | solution.py:133
  24.8 86.6 %copy-start.2 = (bf16[64,2560]{1,0:T(8,128)(2,1)S(1)}, bf16[64,2560]{1,0:T(8,128)(2,1)}, u32[]{:S(2)}) copy-start(bf16[64,2560]{1,0:T(8,128)(2,1)} %param.10) | copy-start | bytes 983044
  111.4 8.5 %copy-start.1 = (bf16[2560,2560]{1,0:T(8,128)(2,1)S(1)}, bf16[2560,2560]{1,0:T(8,128)(2,1)}, u32[]{:S(2)}) copy-start(bf16[2560,2560]{1,0:T(8,128)(2,1)} %all-gather.3.cloned.1.call-done) | copy-start | bytes 39321604
  119.9 2.6 copy-start.14
  129.8 88.6 %copy-start.15 = (f32[2560]{0:T(1024)S(1)}, f32[2560]{0:T(1024)}, u32[]{:S(2)}) copy-start(f32[2560]{0:T(1024)} %param.18) | copy-start | bytes 30724
  220.6 1.1 copy-start.4
  220.6 1.4 copy-start.5
  220.6 1.6 copy-start.6
  220.6 1.8 copy-start.7
  224.2 1.0 copy-start.10
  226.1 7.8 %collective-permute-start = (bf16[2,64,2560]{2,1,0:T(8,128)(2,1)}, bf16[2,64,2560]{2,1,0:T(8,128)(2,1)S(1)}, u32[]{:S(2)}, u32[]{:S(2)}) collective-permute-start(bf16[2,64,2560]{2,1,0:T(8,128)(2,1)} %pad_maximum_fusion.12), channel_id=1, source_target_pairs={{0,1},{1,2},{2,3},{3,4},{4,5},{5,6},{6,7},{7,8},{8,9},{9,10},{10,1... | collective-permute-start | bytes 1966088 | tf_op jit(solution)/shard_map/ppermute | solution.py:23
  229.7 18.8 %collective-permute-start.1 = (bf16[2,64,2560]{2,1,0:T(8,128)(2,1)}, bf16[2,64,2560]{2,1,0:T(8,128)(2,1)}, u32[]{:S(2)}, u32[]{:S(2)}) collective-permute-start(bf16[2,64,2560]{2,1,0:T(8,128)(2,1)} %pad_maximum_fusion.12), channel_id=1, source_target_pairs={{0,2},{1,3},{2,4},{3,5},{4,6},{5,7},{6,8},{7,9},{8,10},{9,11},{10,... | collective-permute-start | bytes 1966088 | tf_op jit(solution)/shard_map/ppermute | solution.py:23
  251.5 2.1 copy-start.16
  252.5 1.1 copy-start.11
  253.6 3.5 %copy-start.13 = (bf16[64,20,128]{2,0,1:T(8,128)(2,1)}, bf16[64,20,128]{2,0,1:T(8,128)(2,1)S(1)}, u32[]{:S(2)}) copy-start(bf16[64,20,128]{2,0,1:T(8,128)(2,1)S(1)} %copy.26) | copy-start | bytes 983044
  253.6 3.5 %copy-start.12 = (bf16[64,20,128]{2,0,1:T(8,128)(2,1)S(1)}, bf16[64,20,128]{2,0,1:T(8,128)(2,1)}, u32[]{:S(2)}) copy-start(bf16[64,20,128]{2,0,1:T(8,128)(2,1)} %copy.25) | copy-start | bytes 983044
  280.9 1.1 copy-start.8
  280.9 1.4 copy-start.9
Sparse Core Ops, SparseCore 0:
  10.2 101.1 all-gather.2
  114.3 96.7 all-gather.4
where the time goes:
time: 301 us; the launch traced here: 296 us
  waiting for transfers between devices  181 us (60%)
  matrix products  43.8 us (15%)
  local copies, waits for them, and re-layouts  26.6 us (9%)
  between operations  19.8 us (7%)
  other arithmetic  19.1 us (6%)
  starting transfers between devices  6.37 us (2%)
    all_gather x1, waiting for transfers between devices, local(): lax.all_gather(w_key, 'fsdp', axis=0, tiled=True)  84.5 us
    all_gather x1, waiting for transfers between devices, local(): lax.all_gather(w_query, 'fsdp', axis=0, tiled=True)  81.3 us
    ppermute x2, waiting for transfers between devices, passed_along(): lax.ppermute(value, axis, [(source, source + steps) for source in range(l...  13.6 us
    dot_general x1, matrix products, absorb_both(): jnp.dot(noisy_hidden, pieces[1], preferred_element_type=jnp.float32)  7.44 us
    dot_general x1, matrix products, absorb_both(): jnp.dot(noisy_hidden, pieces[0], preferred_element_type=jnp.float32)  7.28 us
    dot_general x1, matrix products, local(): query_raw = jnp.dot(hidden, full_query, preferred_element_type=jnp.float32)  7.28 us
    dot_general x1, matrix products, local(): key_raw = jnp.dot(hidden, full_key, preferred_element_type=jnp.float32)  7.28 us
    sub x2, matrix products, attend(): expanded = jnp.exp(scores - highest)  6.65 us
  transfers between devices with their start and end apart: 4, of which 3 were waited for; matrix products, arithmetic and copies ran while one was open for 11% of the time, Pallas kernels for 0%

commit v1 on v0

--- a/solution.py
+++ b/solution.py
@@ -1,8 +1,11 @@
+import functools
 import math
 
 import jax
 import jax.numpy as jnp
 from jax import lax
+from jax.experimental import pallas as pl
+from jax.experimental.pallas import tpu as pltpu
 from jax.sharding import PartitionSpec as P
 
 HEADS = 20
@@ -179,6 +182,385 @@
     return latent
 
 
+TEAM = 4
+MESH = pl.DeviceIdType.MESH
+
+
+def fused_kernel(
+    count, bias_ref, feat_ref, sig_ref, cos_ref, sin_ref, noisy_ref, clean_ref, wq_ref, wk_ref,
+    proj_ref, qg_ref, kg_ref, out_ref,
+    w_all, hid, hid2, ctx_k, ctx_v, qk_raw, ck_raw, stat, mix, mix_out, latent, mods, q_rows, k_rows,
+    bias_all, send_sem, recv_sem, local_sem,
+):
+    rows, width = noisy_ref.shape
+    part = wq_ref.shape[0]
+    inner = wq_ref.shape[1] // TEAM
+    heads = inner // HEAD_DIM
+    groups = count // TEAM
+    half = groups // 2
+    me = lax.axis_index("fsdp")
+    group = me // TEAM
+    rank = me % TEAM
+    sib_rank = rank + 1 - 2 * (rank % 2)
+    far_rank = (rank + 2) % TEAM
+    diag_rank = (sib_rank + 2) % TEAM
+    ranks = [rank, sib_rank, far_rank, diag_rank]
+    low = group % 2
+    spot = group // 2 + low * (groups - 1 - 2 * (group // 2))
+
+    def group_at(place):
+        place = (place + 2 * groups) % groups
+        upper = place // half
+        return 2 * (place + upper * (groups - 1 - 2 * place)) + upper
+
+    base = group * TEAM
+    peers = [base + r for r in ranks]
+    ring_next = group_at(spot + 1) * TEAM + rank
+    ring_prev = group_at(spot - 1) * TEAM + rank
+    later = ((group + 1) % groups) * TEAM + rank
+    earlier = ((group + groups - 1) % groups) * TEAM + rank
+
+    def cols(r):
+        return pl.ds(pl.multiple_of(r * inner, 128), inner)
+
+    def wrows(device):
+        return pl.ds(pl.multiple_of(device * part, 16), part)
+
+    barrier = pltpu.get_barrier_semaphore()
+    friends = peers[1:] + [ring_next, ring_prev, later, earlier]
+    for friend in friends:
+        pl.semaphore_signal(barrier, inc=1, device_id={"fsdp": friend}, device_id_type=MESH)
+
+    own = [
+        pltpu.make_async_copy(
+            ref.at[:, cols(rank)], w_all.at[wrows(me), pl.ds(k * inner, inner)], local_sem.at[k]
+        )
+        for k, ref in enumerate((wq_ref, wk_ref))
+    ]
+    for copy in own:
+        copy.start()
+    for copy in own:
+        copy.wait()
+    pl.semaphore_wait(barrier, len(friends))
+
+    used = [0]
+    started = []
+
+    def remote(src, dst, target):
+        index = used[0]
+        used[0] += 1
+        copy = pltpu.make_async_remote_copy(
+            src_ref=src, dst_ref=dst, send_sem=send_sem.at[index], recv_sem=recv_sem.at[index],
+            device_id={"fsdp": target}, device_id_type=MESH,
+        )
+        return copy, index
+
+    def go(copy):
+        copy[0].start()
+        started.append(copy[0])
+
+    def landing(copy, dst):
+        return pltpu.make_async_remote_copy(
+            src_ref=dst, dst_ref=dst, send_sem=send_sem.at[copy[1]],
+            recv_sem=recv_sem.at[copy[1]], device_id={"fsdp": peers[1]}, device_id_type=MESH,
+        )
+
+    def ring_send(step, slot):
+        arrivals = []
+        for sign, target in ((1, ring_next), (-1, ring_prev)):
+            lanes = pl.ds(0, 2 * inner)
+            if step == half - 1:
+                lanes = pl.ds(0, inner) if sign == 1 else pl.ds(inner, inner)
+            source = group_at(spot - sign * step) * TEAM + ranks[slot]
+            view = w_all.at[wrows(source), lanes]
+            copy = remote(view, view, target)
+            go(copy)
+            coming = group_at(spot - sign * (step + 1)) * TEAM + ranks[slot]
+            arrivals.append((copy, w_all.at[wrows(coming), lanes]))
+        return arrivals
+
+    ring = {}
+    ring[0, 0] = ring_send(0, 0)
+    scatter = {}
+    for slot in range(1, TEAM):
+        for k, ref in enumerate((wq_ref, wk_ref)):
+            lanes = pl.ds(k * inner, inner)
+            copy = remote(ref.at[:, cols(ranks[slot])], w_all.at[wrows(me), lanes], peers[slot])
+            go(copy)
+            scatter[slot, k] = (copy, w_all.at[wrows(peers[slot]), lanes])
+
+    mods[...] = jnp.dot(feat_ref[...], proj_ref[...], preferred_element_type=jnp.float32)
+
+    def modulated(values, index):
+        centred = values - jnp.mean(values, axis=-1, keepdims=True)
+        variance = jnp.mean(centred * centred, axis=-1, keepdims=True)
+        normed = centred * lax.rsqrt(variance + EPSILON)
+        scale = mods[index : index + 1, width : 2 * width]
+        return (normed * (1.0 + scale) + mods[index : index + 1, :width]).astype(jnp.bfloat16)
+
+    def share(buffer, lead):
+        own_view = buffer.at[lead + (rank,)]
+        to_sib = remote(own_view, own_view, peers[1])
+        to_far = remote(own_view, own_view, peers[2])
+        go(to_far)
+        go(to_sib)
+        return (
+            landing(to_sib, buffer.at[lead + (sib_rank,)]),
+            landing(to_far, buffer.at[lead + (far_rank,)]),
+        )
+
+    def share_rest(buffer, lead, pending):
+        from_sib, from_far = pending
+        from_far.wait_recv()
+        view = buffer.at[lead + (far_rank,)]
+        forward = remote(view, view, peers[1])
+        go(forward)
+        from_sib.wait_recv()
+        landing(forward, buffer.at[lead + (diag_rank,)]).wait_recv()
+
+    def share_all(buffer, lead):
+        waits = []
+        view = buffer.at[lead + (rank,)]
+        for slot in (2, 3, 1):
+            copy = remote(view, view, peers[slot])
+            go(copy)
+            waits.append(landing(copy, buffer.at[lead + (ranks[slot],)]))
+        return waits
+
+    latent[...] = noisy_ref[...].astype(jnp.float32)
+    hid[0, pl.ds(rank, 1)] = modulated(latent[...], 1)[None]
+    pending_noisy = share(hid, (0,))
+    hid[1, pl.ds(rank, 1)] = modulated(clean_ref[...].astype(jnp.float32), 0)[None]
+    pending_clean = share(hid, (1,))
+    bias_all[pl.ds(rank, 1)] = bias_ref[...][None]
+    pending_bias = share_all(bias_all, ())
+
+    for slot in range(1, TEAM):
+        for k in range(2):
+            copy, view = scatter[slot, k]
+            landing(copy, view).wait_recv()
+        ring[0, slot] = ring_send(0, slot)
+
+    share_rest(hid, (0,), pending_noisy)
+    share_rest(hid, (1,), pending_clean)
+    for wait in pending_bias:
+        wait.wait_recv()
+
+    for s in range(TEAM):
+        ctx_v[LAGS + s] = hid[1, s, :, cols(rank)]
+    v_copy = remote(ctx_v.at[pl.ds(TEAM, LAGS)], ctx_v.at[pl.ds(0, LAGS)], later)
+    go(v_copy)
+
+    for step in range(1, half):
+        for slot in range(TEAM):
+            for copy, view in ring[step - 1, slot]:
+                landing(copy, view).wait_recv()
+            ring[step, slot] = ring_send(step, slot)
+    for slot in range(TEAM):
+        for copy, view in ring[half - 1, slot]:
+            landing(copy, view).wait_recv()
+    landing(v_copy, ctx_v.at[pl.ds(0, LAGS)]).wait_recv()
+
+    all_rows = TEAM * rows
+
+    def project(source, first, last, target):
+        start = first
+        while start < last:
+            size = min(256, last - start)
+            target[:, start - first : start - first + size] = jnp.dot(
+                source, w_all[:, start : start + size], preferred_element_type=jnp.float32
+            )
+            start += size
+
+    ones = jnp.ones((8, inner), jnp.float32)
+    nt = (((1,), (1,)), ((), ()))
+
+    def squares(values):
+        return lax.dot_general(
+            ones, values * values, nt, precision=lax.Precision.HIGHEST,
+            preferred_element_type=jnp.float32,
+        )
+
+    def row_scale(sums, index):
+        pick = (lax.broadcasted_iota(jnp.int32, (8, 128), 0) == index).astype(jnp.float32)
+        total = lax.dot_general(
+            sums, pick, (((0,), (0,)), ((), ())), precision=lax.Precision.HIGHEST,
+            preferred_element_type=jnp.float32,
+        )
+        return lax.rsqrt(total * (1.0 / width) + EPSILON)
+
+    def turn(values, scale, gain_ref, h):
+        gain = gain_ref[:, pl.ds(pl.multiple_of(rank * inner + h * HEAD_DIM, 128), HEAD_DIM)]
+        value = values * scale * gain
+        rolled = pltpu.roll(value, HEAD_DIM // 2, 1)
+        return (value * cos_ref[...] + rolled * sin_ref[...]).astype(jnp.bfloat16)
+
+    for step in range(STEPS):
+        buffer = hid if step == 0 else hid2
+        if step == 1:
+            hid2[0, pl.ds(rank, 1)] = modulated(latent[...], 2)[None]
+            share_rest(hid2, (0,), share(hid2, (0,)))
+        rows_in = buffer[0].reshape(all_rows, width)
+        project(rows_in, 0, 2 * inner, qk_raw)
+        if step == 0:
+            project(hid[1].reshape(all_rows, width), inner, 2 * inner, ck_raw)
+        row_kind = lax.broadcasted_iota(jnp.int32, (8, all_rows), 0)
+        sums = jnp.where(
+            row_kind == 0, squares(qk_raw[:, :inner]), squares(qk_raw[:, inner:])
+        )
+        if step == 0:
+            sums = jnp.where(row_kind == 2, squares(ck_raw[...]), sums)
+        stat[step, pl.ds(rank, 1)] = sums[None]
+        for wait in share_all(stat, (step,)):
+            wait.wait_recv()
+        total = stat[step, 0] + stat[step, 1] + stat[step, 2] + stat[step, 3]
+        if step == 0:
+            c_scale = row_scale(total, 2)
+            for h in range(heads):
+                lanes = slice(h * HEAD_DIM, (h + 1) * HEAD_DIM)
+                turned = turn(ck_raw[:, lanes], c_scale, kg_ref, h)
+                ctx_k[LAGS : LAGS + TEAM, :, lanes] = turned.reshape(TEAM, rows, HEAD_DIM)
+            k_copy = remote(ctx_k.at[pl.ds(TEAM, LAGS)], ctx_k.at[pl.ds(0, LAGS)], later)
+            go(k_copy)
+        q_scale = row_scale(total, 0)
+        k_scale = row_scale(total, 1)
+        for h in range(heads):
+            lanes = slice(h * HEAD_DIM, (h + 1) * HEAD_DIM)
+            q_rows[:, lanes] = turn(qk_raw[:, lanes], q_scale, qg_ref, h)
+            k_lanes = slice(inner + h * HEAD_DIM, inner + (h + 1) * HEAD_DIM)
+            k_rows[:, lanes] = turn(qk_raw[:, k_lanes], k_scale, kg_ref, h)
+        if step == 0:
+            landing(k_copy, ctx_k.at[pl.ds(0, LAGS)]).wait_recv()
+        for s in range(TEAM):
+            span = slice(s * rows, (s + 1) * rows)
+            for h in range(heads):
+                lanes = slice(h * HEAD_DIM, (h + 1) * HEAD_DIM)
+                query = q_rows[span, lanes]
+                keys = ctx_k[s : s + LAGS, :, lanes].reshape(LAGS * rows, HEAD_DIM)
+                values = ctx_v[s : s + LAGS, :, lanes].reshape(LAGS * rows, HEAD_DIM)
+                own_values = buffer[
+                    0, s, :, pl.ds(pl.multiple_of(rank * inner + h * HEAD_DIM, 128), HEAD_DIM)
+                ]
+                near = lax.dot_general(
+                    query, k_rows[span, lanes], nt, preferred_element_type=jnp.float32
+                ) * HEAD_DIM ** (-0.5)
+                past = lax.dot_general(
+                    query, keys, nt, preferred_element_type=jnp.float32
+                ) * HEAD_DIM ** (-0.5) + bias_all[s, 0:1, :]
+                highest = jnp.maximum(
+                    jnp.max(near, axis=-1, keepdims=True), jnp.max(past, axis=-1, keepdims=True)
+                )
+                near = jnp.exp(near - highest)
+                past = jnp.exp(past - highest)
+                inverse = 1.0 / (
+                    jnp.sum(near, axis=-1, keepdims=True) + jnp.sum(past, axis=-1, keepdims=True)
+                )
+                mixed = jnp.dot(
+                    (near * inverse).astype(jnp.bfloat16), own_values,
+                    preferred_element_type=jnp.float32,
+                ) + jnp.dot(
+                    (past * inverse).astype(jnp.bfloat16), values,
+                    preferred_element_type=jnp.float32,
+                )
+                mix_out[step, s, :, lanes] = mixed.astype(jnp.bfloat16)
+        waits = []
+        for slot in (2, 3, 1):
+            copy = remote(mix_out.at[step, ranks[slot]], mix.at[step, rank], peers[slot])
+            go(copy)
+            waits.append(landing(copy, mix.at[step, ranks[slot]]))
+        mix[step, pl.ds(rank, 1)] = mix_out[step, pl.ds(rank, 1)]
+        for wait in waits:
+            wait.wait_recv()
+        change = sig_ref[step]
+        for r in range(TEAM):
+            lanes = slice(r * inner, (r + 1) * inner)
+            gate = mods[step + 1 : step + 2, 2 * width + r * inner : 2 * width + (r + 1) * inner]
+            fresh = (
+                latent[:, lanes] + (change * gate) * mix[step, r].astype(jnp.float32)
+            ).astype(jnp.bfloat16)
+            if step == STEPS - 1:
+                out_ref[:, lanes] = fresh
+            else:
+                latent[:, lanes] = fresh.astype(jnp.float32)
+
+    for copy in started:
+        copy.wait_send()
+
+
+def fused(noisy, clean, seg_ids, lag_mask, plan, w_query, w_key, time_proj, q_gain, k_gain):
+    rows, width = noisy.shape
+    inner = w_query.shape[1] // TEAM
+    count = lax.axis_size("fsdp")
+    me = lax.axis_index("fsdp")
+    spans = (me // TEAM) * TEAM + jnp.arange(TEAM, dtype=jnp.int32)
+    starts = jnp.sum((seg_ids[None, :] < seg_ids[spans][:, None]).astype(jnp.int32), axis=1)
+    positions = (
+        (spans - starts)[:, None] * rows + jnp.arange(rows, dtype=jnp.int32)[None, :]
+    ).reshape(-1).astype(jnp.float32)
+    half_count = HEAD_DIM // 2
+    angles = positions[:, None] * frequencies(half_count)[None, :]
+    cosine, sine = jnp.cos(angles), jnp.sin(angles)
+    cosine = jnp.concatenate([cosine, cosine], axis=1)
+    sine = jnp.concatenate([-sine, sine], axis=1)
+    levels = sigma_of(plan[0])
+    sigmas = jnp.concatenate([jnp.zeros((1,), jnp.float32), levels, jnp.zeros((5,), jnp.float32)])
+    turns = 1000.0 * sigmas[:, None] * frequencies(time_proj.shape[0] // 2)[None, :]
+    features = jnp.concatenate([jnp.cos(turns), jnp.sin(turns)], axis=1).astype(jnp.bfloat16)
+    changes = jnp.concatenate([levels[1:], jnp.zeros((1,), jnp.float32)]) - levels
+    pieces = []
+    for distance in range(LAGS, 0, -1):
+        source = jnp.maximum(me - distance, 0)
+        allowed = (
+            (me >= distance)
+            & (seg_ids[source] == seg_ids[me])
+            & (lag_mask[0, distance - 1] == 1)
+        )
+        pieces.append(jnp.full((rows,), jnp.where(allowed, 0.0, MASKED), jnp.float32))
+    bias = jnp.broadcast_to(jnp.concatenate(pieces)[None, :], (8, LAGS * rows))
+    vmem = pl.BlockSpec(memory_space=pltpu.VMEM)
+    total = TEAM * rows
+    bf16, f32 = jnp.bfloat16, jnp.float32
+    copies = 96 + 4 * count
+    return pl.pallas_call(
+        functools.partial(fused_kernel, count),
+        out_shape=jax.ShapeDtypeStruct(noisy.shape, bf16),
+        in_specs=[vmem, vmem, pl.BlockSpec(memory_space=pltpu.SMEM)] + [vmem] * 9,
+        out_specs=vmem,
+        scratch_shapes=[
+            pltpu.VMEM((width, 2 * inner), bf16),
+            pltpu.VMEM((2, TEAM, rows, width), bf16),
+            pltpu.VMEM((1, TEAM, rows, width), bf16),
+            pltpu.VMEM((LAGS + TEAM, rows, inner), bf16),
+            pltpu.VMEM((LAGS + TEAM, rows, inner), bf16),
+            pltpu.VMEM((total, 2 * inner), f32),
+            pltpu.VMEM((total, inner), f32),
+            pltpu.VMEM((STEPS, TEAM, 8, total), f32),
+            pltpu.VMEM((STEPS, TEAM, rows, inner), bf16),
+            pltpu.VMEM((STEPS, TEAM, rows, inner), bf16),
+            pltpu.VMEM((rows, width), f32),
+            pltpu.VMEM((8, 3 * width), f32),
+            pltpu.VMEM((total, inner), bf16),
+            pltpu.VMEM((total, inner), bf16),
+            pltpu.VMEM((TEAM, 8, LAGS * rows), f32),
+            pltpu.SemaphoreType.DMA((copies,)),
+            pltpu.SemaphoreType.DMA((copies,)),
+            pltpu.SemaphoreType.DMA((2,)),
+        ],
+        compiler_params=pltpu.CompilerParams(
+            collective_id=0, has_side_effects=True, vmem_limit_bytes=48 * 1024 * 1024
+        ),
+    )(
+        bias, features, changes, cosine, sine, noisy, clean, w_query, w_key, time_proj,
+        q_gain[None, :], k_gain[None, :],
+    )
+
+
+def body(*arrays):
+    part = arrays[5].shape[0]
+    aligned = lax.axis_size("fsdp") % (2 * TEAM) == 0 and part % 16 == 0
+    return (fused if aligned else local)(*arrays)
+
+
 def solution(mesh):
     placed = (
         P(("pool", "fsdp"), None),
@@ -193,5 +575,5 @@
         P(),
     )
     return jax.shard_map(
-        local, mesh=mesh, in_specs=placed, out_specs=P(("pool", "fsdp"), None), check_vma=False
+        body, mesh=mesh, in_specs=placed, out_specs=P(("pool", "fsdp"), None), check_vma=False
     )

time: 301 us -> 158 us (0.52); the launches traced: 296 us -> 157 us
  waiting for transfers between devices: 181 us -> 0 us
  Pallas kernels: 0 us -> 140 us
  matrix products: 43.8 us -> 0 us
  local copies, waits for them, and re-layouts: 26.6 us -> 8.6 us
  between operations: 19.8 us -> 3.86 us
  other arithmetic: 19.1 us -> 4.58 us
  starting transfers between devices: 6.37 us -> 0 us
    all_gather x2 -> x0, waiting for transfers between devices: 166 us -> none  [the longest x1 84.5 us: local(): lax.all_gather(w_key, 'fsdp', axis=0, tiled=True)]
    pallas_call x0 -> x1, Pallas kernels: none -> 140 us  [fused(): pl.pallas_call(functools.partial(fused_kernel, count), out_shape=jax.Shap...]
    dot_general x10 -> x0, matrix products: 37.1 us -> none  [the longest x1 7.44 us: absorb_both(): jnp.dot(noisy_hidden, pieces[1], preferred_element_type=jnp.float32)]
    ppermute x2 -> x0, waiting for transfers between devices: 13.6 us -> none  [passed_along(): lax.ppermute(value, axis, [(source, source + steps) for source in range(l...]
    slice x9 -> x2, local copies, waits for them, and re-layouts: 10.7 us -> 1.95 us  [the longest x1 1.36 us: fused(): lag_mask[0, distance - 1] == 1]
    sub x2 -> x0, matrix products: 6.65 us -> none  [attend(): expanded = jnp.exp(scores - highest)]
    ppermute x2 -> x0, starting transfers between devices: 6.33 us -> none  [passed_along(): lax.ppermute(value, axis, [(source, source + steps) for source in range(l...]
    reshape x5 -> x0, local copies, waits for them, and re-layouts: 5.72 us -> none  [rotate(): split_heads = values.reshape(values.shape[:-1] + (HEADS, HEAD_DIM))]
  transfers between devices with their start and end apart: 4 -> 0, of which waited for: 3 -> 0; matrix products, arithmetic and copies ran while one was open for 11% -> 0% of each run, Pallas kernels for 0% -> 0%
where the time goes in v1:
time: 158 us; the launch traced here: 157 us
  Pallas kernels  140 us (89%)
  local copies, waits for them, and re-layouts  8.6 us (5%)
  other arithmetic  4.58 us (3%)
  between operations  3.86 us (2%)
    pallas_call x1, Pallas kernels, fused(): pl.pallas_call(functools.partial(fused_kernel, count), out_shape=jax.Shap...  140 us

profile of v1, /device:TPU:0, one launch (start us, length us, event | category | flops | bytes accessed | tf_op | source)
XLA Modules:
  0.0 157.2 jit_solution(4901856009006283279)
XLA Ops:
  0.0 0.0 copy-start.3
  0.0 0.0 copy-start.4
  0.0 0.0 copy-start.1
  0.0 0.0 copy-start.2
  0.0 1.4 gather_fusion
  1.4 0.8 convert_reduce_fusion
  2.3 0.1 add_convert_fusion
  2.4 0.1 convert_element_type.23
  2.5 0.5 fusion
  3.0 0.1 pad_maximum_fusion
  3.2 1.4 fusion.5
  5.8 1.4 fusion.4
  9.7 0.7 fusion.6
  10.4 0.1 maximum_multiply_fusion
  10.5 0.1 fusion.1
  10.6 0.1 pad_maximum_fusion.2.feat_ref
  10.7 0.7 broadcast_in_dim.10.qg_ref
  11.4 0.7 broadcast_in_dim.11.kg_ref
  12.1 0.7 add_divide_fusion
  12.8 0.6 slice.14
  13.4 1.4 maximum_subtract_fusion.sig_ref
  14.7 0.0 copy-done.3
  14.7 0.0 copy-done.4
  14.7 0.0 copy-done.1
  14.7 0.0 copy-done.2
  14.8 0.0 copy-start
  14.8 1.5 copy-done
  16.3 140.1 %shard_map.100 = bf16[64,2560]{1,0:T(8,128)(2,1)S(1)} custom-call(f32[8,128]{1,0:T(8,128)S(1)} %broadcast_in_dim.9.bias_ref, bf16[8,128]{1,0:T(8,128)(2,1)S(1)} %pad_maximum_fusion.2.feat_ref, f32[2]{0:T(128)S(1)} %maximum_subtract_fusion.sig_ref, f32[256,128]{1,0:T(8,128)S(1)} %get-tuple-element.15.cos_ref, f32[256,128]{1,0:T(8,128)S(1)} %get-tuple-element.16.sin_ref, ...), custom_call_target="tpu_custom_call" | custom-call | tf_op jit(solution)/shard_map/pallas_call | solution.py:524
  156.5 0.7 copy.12
  (8 shorter events, 0.0 us)
Async XLA Ops:
  0.0 14.7 %copy-start.3 = (bf16[64,2560]{1,0:T(8,128)(2,1)S(1)}, bf16[64,2560]{1,0:T(8,128)(2,1)}, u32[]{:S(2)}) copy-start(bf16[64,2560]{1,0:T(8,128)(2,1)} %noisy_ref.1) | copy-start | bytes 983044
  0.0 14.7 %copy-start.4 = (bf16[64,2560]{1,0:T(8,128)(2,1)S(1)}, bf16[64,2560]{1,0:T(8,128)(2,1)}, u32[]{:S(2)}) copy-start(bf16[64,2560]{1,0:T(8,128)(2,1)} %clean_ref.1) | copy-start | bytes 983044
  0.0 14.7 %copy-start.1 = (bf16[80,2560]{1,0:T(8,128)(2,1)S(1)}, bf16[80,2560]{1,0:T(8,128)(2,1)}, u32[]{:S(2)}) copy-start(bf16[80,2560]{1,0:T(8,128)(2,1)} %wq_ref.1) | copy-start | bytes 1228804
  0.0 14.7 %copy-start.2 = (bf16[80,2560]{1,0:T(8,128)(2,1)S(1)}, bf16[80,2560]{1,0:T(8,128)(2,1)}, u32[]{:S(2)}) copy-start(bf16[80,2560]{1,0:T(8,128)(2,1)} %wk_ref.1) | copy-start | bytes 1228804
  14.8 1.5 copy-start

commit v2 on v1

--- a/solution.py
+++ b/solution.py
@@ -187,10 +187,10 @@
 
 
 def fused_kernel(
-    count, bias_ref, feat_ref, sig_ref, cos_ref, sin_ref, noisy_ref, clean_ref, wq_ref, wk_ref,
-    proj_ref, qg_ref, kg_ref, out_ref,
+    count, seg_ref, lag_ref, plan_ref, noisy_ref, clean_ref, wq_ref, wk_ref, proj_ref, qg_ref,
+    kg_ref, out_ref,
     w_all, hid, hid2, ctx_k, ctx_v, qk_raw, ck_raw, stat, mix, mix_out, latent, mods, q_rows, k_rows,
-    bias_all, send_sem, recv_sem, local_sem,
+    bias_all, cos_ref, sin_ref, send_sem, recv_sem, local_sem,
 ):
     rows, width = noisy_ref.shape
     part = wq_ref.shape[0]
@@ -289,7 +289,24 @@
             go(copy)
             scatter[slot, k] = (copy, w_all.at[wrows(peers[slot]), lanes])
 
-    mods[...] = jnp.dot(feat_ref[...], proj_ref[...], preferred_element_type=jnp.float32)
+    def lane_frequencies(shape, half_count):
+        lane = lax.broadcasted_iota(jnp.int32, shape, 1) % half_count
+        return jnp.exp(lane.astype(jnp.float32) * (-math.log(10000.0) / half_count))
+
+    def sigma_rows(step):
+        level = jnp.full((8, proj_ref.shape[0]), plan_ref[0, step], jnp.int32)
+        return sigma_of(level)
+
+    steps_sigma = [sigma_rows(step) for step in range(STEPS)]
+    row_at = lax.broadcasted_iota(jnp.int32, steps_sigma[0].shape, 0)
+    sigmas = jnp.zeros(steps_sigma[0].shape, jnp.float32)
+    for step in range(STEPS):
+        sigmas = jnp.where(row_at == step + 1, steps_sigma[step], sigmas)
+    time_half = proj_ref.shape[0] // 2
+    turns = 1000.0 * sigmas * lane_frequencies(sigmas.shape, time_half)
+    first = lax.broadcasted_iota(jnp.int32, sigmas.shape, 1) < time_half
+    features = jnp.where(first, jnp.cos(turns), jnp.sin(turns)).astype(jnp.bfloat16)
+    mods[...] = jnp.dot(features, proj_ref[...], preferred_element_type=jnp.float32)
 
     def modulated(values, index):
         centred = values - jnp.mean(values, axis=-1, keepdims=True)
@@ -327,22 +344,44 @@
             waits.append(landing(copy, buffer.at[lead + (ranks[slot],)]))
         return waits
 
-    latent[...] = noisy_ref[...].astype(jnp.float32)
-    hid[0, pl.ds(rank, 1)] = modulated(latent[...], 1)[None]
-    pending_noisy = share(hid, (0,))
-    hid[1, pl.ds(rank, 1)] = modulated(clean_ref[...].astype(jnp.float32), 0)[None]
-    pending_clean = share(hid, (1,))
-    bias_all[pl.ds(rank, 1)] = bias_ref[...][None]
-    pending_bias = share_all(bias_all, ())
-
-    for slot in range(1, TEAM):
+    def pass_own(slot):
         for k in range(2):
             copy, view = scatter[slot, k]
             landing(copy, view).wait_recv()
         ring[0, slot] = ring_send(0, slot)
 
+    def pass_on(step, slot):
+        if step < half:
+            for copy, view in ring[step - 1, slot]:
+                landing(copy, view).wait_recv()
+            ring[step, slot] = ring_send(step, slot)
+
+    pass_own(1)
+    latent[...] = noisy_ref[...].astype(jnp.float32)
+    hid[0, pl.ds(rank, 1)] = modulated(latent[...], 1)[None]
+    pending_noisy = share(hid, (0,))
+    pass_on(1, 0)
+    pass_own(2)
+    pass_own(3)
+    hid[1, pl.ds(rank, 1)] = modulated(clean_ref[...].astype(jnp.float32), 0)[None]
+    pending_clean = share(hid, (1,))
+    here = seg_ref[me]
+    bias_lane = lax.broadcasted_iota(jnp.int32, (8, LAGS * rows), 1) // rows
+    bias = jnp.zeros((8, LAGS * rows), jnp.float32)
+    for distance in range(1, LAGS + 1):
+        source = jnp.maximum(me - distance, 0)
+        level = jnp.where(seg_ref[source] == here, 0.0, MASKED)
+        level = jnp.where(lag_ref[0, distance - 1] == 1, level, MASKED)
+        level = jnp.where(me >= distance, level, MASKED)
+        bias = jnp.where(bias_lane == LAGS - distance, level, bias)
+    bias_all[pl.ds(rank, 1)] = bias[None]
+    pending_bias = share_all(bias_all, ())
+    pass_on(1, 1)
+    pass_on(1, 2)
     share_rest(hid, (0,), pending_noisy)
+    pass_on(1, 3)
     share_rest(hid, (1,), pending_clean)
+    pass_on(2, 0)
     for wait in pending_bias:
         wait.wait_recv()
 
@@ -350,12 +389,27 @@
         ctx_v[LAGS + s] = hid[1, s, :, cols(rank)]
     v_copy = remote(ctx_v.at[pl.ds(TEAM, LAGS)], ctx_v.at[pl.ds(0, LAGS)], later)
     go(v_copy)
-
-    for step in range(1, half):
+    for slot in range(1, TEAM):
+        pass_on(2, slot)
+
+    half_count = HEAD_DIM // 2
+    for s in range(TEAM):
+        span_id = seg_ref[base + s]
+        start = jnp.int32(0)
+        for other in range(count):
+            start = start + jnp.where(seg_ref[other] < span_id, 1, 0)
+        place = (base + s - start) * rows
+        shape = (rows, HEAD_DIM)
+        position = (lax.broadcasted_iota(jnp.int32, shape, 0) + place).astype(jnp.float32)
+        angles = position * lane_frequencies(shape, half_count)
+        sine = jnp.sin(angles)
+        front = lax.broadcasted_iota(jnp.int32, shape, 1) < half_count
+        cos_ref[s * rows : (s + 1) * rows] = jnp.cos(angles)
+        sin_ref[s * rows : (s + 1) * rows] = jnp.where(front, -sine, sine)
+
+    for step in range(3, half):
         for slot in range(TEAM):
-            for copy, view in ring[step - 1, slot]:
-                landing(copy, view).wait_recv()
-            ring[step, slot] = ring_send(step, slot)
+            pass_on(step, slot)
     for slot in range(TEAM):
         for copy, view in ring[half - 1, slot]:
             landing(copy, view).wait_recv()
@@ -390,8 +444,8 @@
         return lax.rsqrt(total * (1.0 / width) + EPSILON)
 
     def turn(values, scale, gain_ref, h):
-        gain = gain_ref[:, pl.ds(pl.multiple_of(rank * inner + h * HEAD_DIM, 128), HEAD_DIM)]
-        value = values * scale * gain
+        gain = gain_ref[pl.ds(pl.multiple_of(rank * inner + h * HEAD_DIM, 128), HEAD_DIM)]
+        value = values * scale * gain[None, :]
         rolled = pltpu.roll(value, HEAD_DIM // 2, 1)
         return (value * cos_ref[...] + rolled * sin_ref[...]).astype(jnp.bfloat16)
 
@@ -471,7 +525,9 @@
         mix[step, pl.ds(rank, 1)] = mix_out[step, pl.ds(rank, 1)]
         for wait in waits:
             wait.wait_recv()
-        change = sig_ref[step]
+        change = -steps_sigma[step][:1, :1]
+        if step + 1 < STEPS:
+            change = change + steps_sigma[step + 1][:1, :1]
         for r in range(TEAM):
             lanes = slice(r * inner, (r + 1) * inner)
             gate = mods[step + 1 : step + 2, 2 * width + r * inner : 2 * width + (r + 1) * inner]
@@ -491,32 +547,6 @@
     rows, width = noisy.shape
     inner = w_query.shape[1] // TEAM
     count = lax.axis_size("fsdp")
-    me = lax.axis_index("fsdp")
-    spans = (me // TEAM) * TEAM + jnp.arange(TEAM, dtype=jnp.int32)
-    starts = jnp.sum((seg_ids[None, :] < seg_ids[spans][:, None]).astype(jnp.int32), axis=1)
-    positions = (
-        (spans - starts)[:, None] * rows + jnp.arange(rows, dtype=jnp.int32)[None, :]
-    ).reshape(-1).astype(jnp.float32)
-    half_count = HEAD_DIM // 2
-    angles = positions[:, None] * frequencies(half_count)[None, :]
-    cosine, sine = jnp.cos(angles), jnp.sin(angles)
-    cosine = jnp.concatenate([cosine, cosine], axis=1)
-    sine = jnp.concatenate([-sine, sine], axis=1)
-    levels = sigma_of(plan[0])
-    sigmas = jnp.concatenate([jnp.zeros((1,), jnp.float32), levels, jnp.zeros((5,), jnp.float32)])
-    turns = 1000.0 * sigmas[:, None] * frequencies(time_proj.shape[0] // 2)[None, :]
-    features = jnp.concatenate([jnp.cos(turns), jnp.sin(turns)], axis=1).astype(jnp.bfloat16)
-    changes = jnp.concatenate([levels[1:], jnp.zeros((1,), jnp.float32)]) - levels
-    pieces = []
-    for distance in range(LAGS, 0, -1):
-        source = jnp.maximum(me - distance, 0)
-        allowed = (
-            (me >= distance)
-            & (seg_ids[source] == seg_ids[me])
-            & (lag_mask[0, distance - 1] == 1)
-        )
-        pieces.append(jnp.full((rows,), jnp.where(allowed, 0.0, MASKED), jnp.float32))
-    bias = jnp.broadcast_to(jnp.concatenate(pieces)[None, :], (8, LAGS * rows))
     vmem = pl.BlockSpec(memory_space=pltpu.VMEM)
     total = TEAM * rows
     bf16, f32 = jnp.bfloat16, jnp.float32
@@ -524,7 +554,7 @@
     return pl.pallas_call(
         functools.partial(fused_kernel, count),
         out_shape=jax.ShapeDtypeStruct(noisy.shape, bf16),
-        in_specs=[vmem, vmem, pl.BlockSpec(memory_space=pltpu.SMEM)] + [vmem] * 9,
+        in_specs=[pl.BlockSpec(memory_space=pltpu.SMEM)] * 3 + [vmem] * 7,
         out_specs=vmem,
         scratch_shapes=[
             pltpu.VMEM((width, 2 * inner), bf16),
@@ -542,6 +572,8 @@
             pltpu.VMEM((total, inner), bf16),
             pltpu.VMEM((total, inner), bf16),
             pltpu.VMEM((TEAM, 8, LAGS * rows), f32),
+            pltpu.VMEM((total, HEAD_DIM), f32),
+            pltpu.VMEM((total, HEAD_DIM), f32),
             pltpu.SemaphoreType.DMA((copies,)),
             pltpu.SemaphoreType.DMA((copies,)),
             pltpu.SemaphoreType.DMA((2,)),
@@ -550,8 +582,7 @@
             collective_id=0, has_side_effects=True, vmem_limit_bytes=48 * 1024 * 1024
         ),
     )(
-        bias, features, changes, cosine, sine, noisy, clean, w_query, w_key, time_proj,
-        q_gain[None, :], k_gain[None, :],
+        seg_ids, lag_mask, plan, noisy, clean, w_query, w_key, time_proj, q_gain, k_gain,
     )
 
 

time: 158 us -> 142 us (0.90)
  Pallas kernels: 140 us -> 132 us
  other arithmetic: 4.58 us -> 0 us
  between operations: 3.86 us -> 0.02 us
    pallas_call x1, Pallas kernels: 140 us -> 132 us  [fused(): pl.pallas_call(functools.partial(fused_kernel, count), out_shape=jax.Shap...]
    unnamed x11 -> x21, local copies, waits for them, and re-layouts: 2.28 us -> 9.59 us
    slice x2 -> x0, local copies, waits for them, and re-layouts: 1.95 us -> none  [the longest x1 1.36 us: fused(): lag_mask[0, distance - 1] == 1]
where the time goes in v2:
time: 142 us; the launch traced here: 141 us
  Pallas kernels  132 us (93%)
  local copies, waits for them, and re-layouts  9.59 us (7%)
    pallas_call x1, Pallas kernels, fused(): pl.pallas_call(functools.partial(fused_kernel, count), out_shape=jax.Shap...  132 us
    unnamed x21, local copies, waits for them, and re-layouts  9.59 us

profile of v2, /device:TPU:0, one launch (start us, length us, event | category | flops | bytes accessed | tf_op | source)
XLA Modules:
  0.0 141.4 jit_solution(796988676393488722)
XLA Ops:
  0.0 0.0 copy-start
  0.0 1.5 %copy-done = bf16[128,7680]{1,0:T(8,128)(2,1)S(1)} copy-done((bf16[128,7680]{1,0:T(8,128)(2,1)S(1)}, bf16[128,7680]{1,0:T(8,128)(2,1)}, u32[]{:S(2)}) %copy-start) | copy-done | bytes 1966104
  1.5 0.0 copy-start.1
  1.5 1.0 copy-done.1
  2.5 0.0 copy-start.2
  2.6 1.0 copy-done.2
  3.6 0.0 copy-start.3
  3.6 1.0 copy-done.3
  4.5 0.0 copy-start.4
  4.5 1.0 copy-done.4
  5.5 0.0 copy-start.5
  5.5 0.7 copy-done.5
  6.2 0.0 copy-start.6
  6.2 0.7 copy-done.6
  6.9 0.0 copy-start.7
  6.9 0.7 copy-done.7
  7.6 0.0 copy-start.8
  7.6 0.7 copy-done.8
  8.2 0.0 copy-start.9
  8.2 0.7 copy-done.9
  8.9 131.8 %shard_map.100 = bf16[64,2560]{1,0:T(8,128)(2,1)S(1)} custom-call(s32[32]{0:T(128)S(1)} %copy-done.7, s32[1,2]{1,0:T(1,128)S(1)} %copy-done.8, s32[1,2]{1,0:T(1,128)S(1)} %copy-done.9, bf16[64,2560]{1,0:T(8,128)(2,1)S(1)} %copy-done.3, bf16[64,2560]{1,0:T(8,128)(2,1)S(1)} %copy-done.4, bf16[80,2560]{1,0:T(8,128)(2,1)S(1)} %copy-done.1, ...), custom_call_target="tpu_custom_call" | custom-call | tf_op jit(solution)/shard_map/pallas_call | solution.py:554
  140.7 0.7 copy.12
Async XLA Ops:
  0.0 1.5 %copy-start = (bf16[128,7680]{1,0:T(8,128)(2,1)S(1)}, bf16[128,7680]{1,0:T(8,128)(2,1)}, u32[]{:S(2)}) copy-start(bf16[128,7680]{1,0:T(8,128)(2,1)} %proj_ref.1) | copy-start | bytes 5898244
  1.5 1.0 copy-start.1
  2.5 1.0 copy-start.2
  3.6 1.0 copy-start.3
  4.5 1.0 copy-start.4
  5.5 0.7 copy-start.5
  6.2 0.7 copy-start.6
  6.9 0.7 copy-start.7
  7.6 0.7 copy-start.8
  8.2 0.7 copy-start.9

commit v3 on v2

--- a/solution.py
+++ b/solution.py
@@ -426,12 +426,16 @@
             )
             start += size
 
-    ones = jnp.ones((8, inner), jnp.float32)
+    ones = jnp.ones((8, HEAD_DIM), jnp.float32)
     nt = (((1,), (1,)), ((), ()))
 
     def squares(values):
+        folded = jnp.zeros((all_rows, HEAD_DIM), jnp.float32)
+        for h in range(heads):
+            head = values[:, h * HEAD_DIM : (h + 1) * HEAD_DIM]
+            folded = folded + head * head
         return lax.dot_general(
-            ones, values * values, nt, precision=lax.Precision.HIGHEST,
+            ones, folded, nt, precision=lax.Precision.HIGHEST,
             preferred_element_type=jnp.float32,
         )
 
@@ -443,55 +447,69 @@
         )
         return lax.rsqrt(total * (1.0 / width) + EPSILON)
 
-    def turn(values, scale, gain_ref, h):
+    def turn(target, offset, gain_ref, h):
+        lanes = slice(offset + h * HEAD_DIM, offset + (h + 1) * HEAD_DIM)
         gain = gain_ref[pl.ds(pl.multiple_of(rank * inner + h * HEAD_DIM, 128), HEAD_DIM)]
-        value = values * scale * gain[None, :]
+        value = target[:, lanes] * gain[None, :]
         rolled = pltpu.roll(value, HEAD_DIM // 2, 1)
-        return (value * cos_ref[...] + rolled * sin_ref[...]).astype(jnp.bfloat16)
+        target[:, lanes] = value * cos_ref[...] + rolled * sin_ref[...]
 
     for step in range(STEPS):
         buffer = hid if step == 0 else hid2
         if step == 1:
             hid2[0, pl.ds(rank, 1)] = modulated(latent[...], 2)[None]
             share_rest(hid2, (0,), share(hid2, (0,)))
-        rows_in = buffer[0].reshape(all_rows, width)
-        project(rows_in, 0, 2 * inner, qk_raw)
+        row_kind = lax.broadcasted_iota(jnp.int32, (8, all_rows), 0)
         if step == 0:
             project(hid[1].reshape(all_rows, width), inner, 2 * inner, ck_raw)
-        row_kind = lax.broadcasted_iota(jnp.int32, (8, all_rows), 0)
+            stat[STEPS, pl.ds(rank, 1)] = squares(ck_raw)[None]
+            c_waits = share_all(stat, (STEPS,))
+        project(buffer[0].reshape(all_rows, width), 0, 2 * inner, qk_raw)
         sums = jnp.where(
-            row_kind == 0, squares(qk_raw[:, :inner]), squares(qk_raw[:, inner:])
-        )
+            row_kind == 0, squares(qk_raw.at[:, :inner]), squares(qk_raw.at[:, inner:])
+        )
+        stat[step, pl.ds(rank, 1)] = sums[None]
+        waits = share_all(stat, (step,))
+
+        def summed(index):
+            return stat[index, 0] + stat[index, 1] + stat[index, 2] + stat[index, 3]
+
         if step == 0:
-            sums = jnp.where(row_kind == 2, squares(ck_raw[...]), sums)
-        stat[step, pl.ds(rank, 1)] = sums[None]
-        for wait in share_all(stat, (step,)):
-            wait.wait_recv()
-        total = stat[step, 0] + stat[step, 1] + stat[step, 2] + stat[step, 3]
-        if step == 0:
-            c_scale = row_scale(total, 2)
+            for h in range(heads):
+                turn(ck_raw, 0, kg_ref, h)
+            for wait in c_waits:
+                wait.wait_recv()
+            c_scale = row_scale(summed(STEPS), 0)
             for h in range(heads):
                 lanes = slice(h * HEAD_DIM, (h + 1) * HEAD_DIM)
-                turned = turn(ck_raw[:, lanes], c_scale, kg_ref, h)
+                turned = (ck_raw[:, lanes] * c_scale).astype(jnp.bfloat16)
                 ctx_k[LAGS : LAGS + TEAM, :, lanes] = turned.reshape(TEAM, rows, HEAD_DIM)
             k_copy = remote(ctx_k.at[pl.ds(TEAM, LAGS)], ctx_k.at[pl.ds(0, LAGS)], later)
             go(k_copy)
+        for h in range(heads):
+            turn(qk_raw, 0, qg_ref, h)
+            turn(qk_raw, inner, kg_ref, h)
+        for wait in waits:
+            wait.wait_recv()
+        total = summed(step)
         q_scale = row_scale(total, 0)
         k_scale = row_scale(total, 1)
         for h in range(heads):
             lanes = slice(h * HEAD_DIM, (h + 1) * HEAD_DIM)
-            q_rows[:, lanes] = turn(qk_raw[:, lanes], q_scale, qg_ref, h)
+            q_rows[:, lanes] = (qk_raw[:, lanes] * q_scale).astype(jnp.bfloat16)
             k_lanes = slice(inner + h * HEAD_DIM, inner + (h + 1) * HEAD_DIM)
-            k_rows[:, lanes] = turn(qk_raw[:, k_lanes], k_scale, kg_ref, h)
+            k_rows[:, lanes] = (qk_raw[:, k_lanes] * k_scale).astype(jnp.bfloat16)
         if step == 0:
             landing(k_copy, ctx_k.at[pl.ds(0, LAGS)]).wait_recv()
-        for s in range(TEAM):
-            span = slice(s * rows, (s + 1) * rows)
+        waits = []
+        for slot in (2, 3, 1, 0):
+            s = ranks[slot]
+            span = pl.ds(pl.multiple_of(s * rows, rows), rows)
             for h in range(heads):
                 lanes = slice(h * HEAD_DIM, (h + 1) * HEAD_DIM)
                 query = q_rows[span, lanes]
-                keys = ctx_k[s : s + LAGS, :, lanes].reshape(LAGS * rows, HEAD_DIM)
-                values = ctx_v[s : s + LAGS, :, lanes].reshape(LAGS * rows, HEAD_DIM)
+                keys = ctx_k[pl.ds(s, LAGS), :, lanes].reshape(LAGS * rows, HEAD_DIM)
+                values = ctx_v[pl.ds(s, LAGS), :, lanes].reshape(LAGS * rows, HEAD_DIM)
                 own_values = buffer[
                     0, s, :, pl.ds(pl.multiple_of(rank * inner + h * HEAD_DIM, 128), HEAD_DIM)
                 ]
@@ -517,11 +535,10 @@
                     preferred_element_type=jnp.float32,
                 )
                 mix_out[step, s, :, lanes] = mixed.astype(jnp.bfloat16)
-        waits = []
-        for slot in (2, 3, 1):
-            copy = remote(mix_out.at[step, ranks[slot]], mix.at[step, rank], peers[slot])
-            go(copy)
-            waits.append(landing(copy, mix.at[step, ranks[slot]]))
+            if slot:
+                copy = remote(mix_out.at[step, s], mix.at[step, rank], peers[slot])
+                go(copy)
+                waits.append(landing(copy, mix.at[step, s]))
         mix[step, pl.ds(rank, 1)] = mix_out[step, pl.ds(rank, 1)]
         for wait in waits:
             wait.wait_recv()
@@ -564,7 +581,7 @@
             pltpu.VMEM((LAGS + TEAM, rows, inner), bf16),
             pltpu.VMEM((total, 2 * inner), f32),
             pltpu.VMEM((total, inner), f32),
-            pltpu.VMEM((STEPS, TEAM, 8, total), f32),
+            pltpu.VMEM((STEPS + 1, TEAM, 8, total), f32),
             pltpu.VMEM((STEPS, TEAM, rows, inner), bf16),
             pltpu.VMEM((STEPS, TEAM, rows, inner), bf16),
             pltpu.VMEM((rows, width), f32),

time: 142 us -> 128 us (0.901)
  Pallas kernels: 132 us -> 118 us
    pallas_call x1, Pallas kernels: 132 us -> 118 us  [fused(): pl.pallas_call(functools.partial(fused_kernel, count), out_shape=jax.Shap...]
where the time goes in v3:
time: 128 us
  Pallas kernels  118 us (92%)
  local copies, waits for them, and re-layouts  9.59 us (7%)
    pallas_call x1, Pallas kernels, fused(): pl.pallas_call(functools.partial(fused_kernel, count), out_shape=jax.Shap...  118 us
    unnamed x21, local copies, waits for them, and re-layouts  9.59 us

profile of v3, /device:TPU:0, one launch (start us, length us, event | category | flops | bytes accessed | tf_op | source)
XLA Modules:
  0.0 127.7 jit_solution(3436709833826530950)
XLA Ops:
  0.0 0.0 copy-start
  0.0 1.5 %copy-done = bf16[128,7680]{1,0:T(8,128)(2,1)S(1)} copy-done((bf16[128,7680]{1,0:T(8,128)(2,1)S(1)}, bf16[128,7680]{1,0:T(8,128)(2,1)}, u32[]{:S(2)}) %copy-start) | copy-done | bytes 1966104
  1.5 0.0 copy-start.1
  1.5 1.0 copy-done.1
  2.5 0.0 copy-start.2
  2.6 1.0 copy-done.2
  3.6 0.0 copy-start.3
  3.6 1.0 copy-done.3
  4.5 0.0 copy-start.4
  4.5 1.0 copy-done.4
  5.5 0.0 copy-start.5
  5.5 0.7 copy-done.5
  6.2 0.0 copy-start.6
  6.2 0.7 copy-done.6
  6.9 0.0 copy-start.7
  6.9 0.7 copy-done.7
  7.6 0.0 copy-start.8
  7.6 0.7 copy-done.8
  8.2 0.0 copy-start.9
  8.2 0.7 copy-done.9
  8.9 118.1 %shard_map.100 = bf16[64,2560]{1,0:T(8,128)(2,1)S(1)} custom-call(s32[32]{0:T(128)S(1)} %copy-done.7, s32[1,2]{1,0:T(1,128)S(1)} %copy-done.8, s32[1,2]{1,0:T(1,128)S(1)} %copy-done.9, bf16[64,2560]{1,0:T(8,128)(2,1)S(1)} %copy-done.3, bf16[64,2560]{1,0:T(8,128)(2,1)S(1)} %copy-done.4, bf16[80,2560]{1,0:T(8,128)(2,1)S(1)} %copy-done.1, ...), custom_call_target="tpu_custom_call" | custom-call | tf_op jit(solution)/shard_map/pallas_call | solution.py:571
  126.9 0.7 copy.12
Async XLA Ops:
  0.0 1.5 %copy-start = (bf16[128,7680]{1,0:T(8,128)(2,1)S(1)}, bf16[128,7680]{1,0:T(8,128)(2,1)}, u32[]{:S(2)}) copy-start(bf16[128,7680]{1,0:T(8,128)(2,1)} %proj_ref.1) | copy-start | bytes 5898244
  1.5 1.0 copy-start.1
  2.5 1.0 copy-start.2
  3.6 1.0 copy-start.3
  4.5 1.0 copy-start.4
  5.5 0.7 copy-start.5
  6.2 0.7 copy-start.6
  6.9 0.7 copy-start.7
  7.6 0.7 copy-start.8
  8.2 0.7 copy-start.9

commit v4 on v3

--- a/solution.py
+++ b/solution.py
@@ -315,25 +315,25 @@
         scale = mods[index : index + 1, width : 2 * width]
         return (normed * (1.0 + scale) + mods[index : index + 1, :width]).astype(jnp.bfloat16)
 
-    def share(buffer, lead):
-        own_view = buffer.at[lead + (rank,)]
+    def share(buffer, lead, lanes=slice(None)):
+        own_view = buffer.at[lead + (rank, slice(None), lanes)]
         to_sib = remote(own_view, own_view, peers[1])
         to_far = remote(own_view, own_view, peers[2])
         go(to_far)
         go(to_sib)
         return (
-            landing(to_sib, buffer.at[lead + (sib_rank,)]),
-            landing(to_far, buffer.at[lead + (far_rank,)]),
-        )
-
-    def share_rest(buffer, lead, pending):
+            landing(to_sib, buffer.at[lead + (sib_rank, slice(None), lanes)]),
+            landing(to_far, buffer.at[lead + (far_rank, slice(None), lanes)]),
+        )
+
+    def share_rest(buffer, lead, pending, lanes=slice(None)):
         from_sib, from_far = pending
         from_far.wait_recv()
-        view = buffer.at[lead + (far_rank,)]
+        view = buffer.at[lead + (far_rank, slice(None), lanes)]
         forward = remote(view, view, peers[1])
         go(forward)
         from_sib.wait_recv()
-        landing(forward, buffer.at[lead + (diag_rank,)]).wait_recv()
+        landing(forward, buffer.at[lead + (diag_rank, slice(None), lanes)]).wait_recv()
 
     def share_all(buffer, lead):
         waits = []
@@ -410,21 +410,36 @@
     for step in range(3, half):
         for slot in range(TEAM):
             pass_on(step, slot)
+    all_rows = TEAM * rows
+    farthest = group_at(spot + half) // 2
+
+    def project(buffer, kind, start, size, first, last, target, fresh):
+        source = buffer[kind, :, :, pl.ds(start, size)].reshape(all_rows, size)
+        left = first
+        while left < last:
+            block = min(256, last - left)
+            product = jnp.dot(
+                source, w_all[pl.ds(start, size), left : left + block],
+                preferred_element_type=jnp.float32,
+            )
+            into = slice(left - first, left - first + block)
+            target[:, into] = product if fresh else target[:, into] + product
+            left += block
+
+    def project_pair(pair, fresh):
+        size = 2 * TEAM * part
+        start = pl.multiple_of(pair * size, 128)
+        project(hid, 1, start, size, inner, 2 * inner, ck_raw, fresh)
+        project(hid, 0, start, size, 0, 2 * inner, qk_raw, fresh)
+
+    for index in range(1, half):
+        project_pair((farthest + index) % half, index == 1)
     for slot in range(TEAM):
         for copy, view in ring[half - 1, slot]:
             landing(copy, view).wait_recv()
+    project_pair(farthest, half == 1)
     landing(v_copy, ctx_v.at[pl.ds(0, LAGS)]).wait_recv()
 
-    all_rows = TEAM * rows
-
-    def project(source, first, last, target):
-        start = first
-        while start < last:
-            size = min(256, last - start)
-            target[:, start - first : start - first + size] = jnp.dot(
-                source, w_all[:, start : start + size], preferred_element_type=jnp.float32
-            )
-            start += size
 
     ones = jnp.ones((8, HEAD_DIM), jnp.float32)
     nt = (((1,), (1,)), ((), ()))
@@ -458,13 +473,16 @@
         buffer = hid if step == 0 else hid2
         if step == 1:
             hid2[0, pl.ds(rank, 1)] = modulated(latent[...], 2)[None]
-            share_rest(hid2, (0,), share(hid2, (0,)))
+            chunk = 2 * inner
+            starts = range(0, width, chunk)
+            pending = [share(hid2, (0,), pl.ds(start, chunk)) for start in starts]
+            for start, flight in zip(starts, pending):
+                share_rest(hid2, (0,), flight, pl.ds(start, chunk))
+                project(hid2, 0, start, chunk, 0, 2 * inner, qk_raw, start == 0)
         row_kind = lax.broadcasted_iota(jnp.int32, (8, all_rows), 0)
         if step == 0:
-            project(hid[1].reshape(all_rows, width), inner, 2 * inner, ck_raw)
             stat[STEPS, pl.ds(rank, 1)] = squares(ck_raw)[None]
             c_waits = share_all(stat, (STEPS,))
-        project(buffer[0].reshape(all_rows, width), 0, 2 * inner, qk_raw)
         sums = jnp.where(
             row_kind == 0, squares(qk_raw.at[:, :inner]), squares(qk_raw.at[:, inner:])
         )

time: 128 us -> 127 us (level)
  Pallas kernels: 118 us -> 116 us
    pallas_call x1, Pallas kernels: 118 us -> 116 us  [fused(): pl.pallas_call(functools.partial(fused_kernel, count), out_shape=jax.Shap...]
where the time goes in v4:
time: 127 us; the launch traced here: 126 us
  Pallas kernels  116 us (91%)
  local copies, waits for them, and re-layouts  9.59 us (8%)
    pallas_call x1, Pallas kernels, fused(): pl.pallas_call(functools.partial(fused_kernel, count), out_shape=jax.Shap...  116 us
    unnamed x21, local copies, waits for them, and re-layouts  9.59 us

profile of v4, /device:TPU:0, one launch (start us, length us, event | category | flops | bytes accessed | tf_op | source)
XLA Modules:
  0.0 126.1 jit_solution(15912593092303528359)
XLA Ops:
  0.0 0.0 copy-start
  0.0 1.5 %copy-done = bf16[128,7680]{1,0:T(8,128)(2,1)S(1)} copy-done((bf16[128,7680]{1,0:T(8,128)(2,1)S(1)}, bf16[128,7680]{1,0:T(8,128)(2,1)}, u32[]{:S(2)}) %copy-start) | copy-done | bytes 1966104
  1.5 0.0 copy-start.1
  1.5 1.0 copy-done.1
  2.5 0.0 copy-start.2
  2.6 1.0 copy-done.2
  3.6 0.0 copy-start.3
  3.6 1.0 copy-done.3
  4.5 0.0 copy-start.4
  4.5 1.0 copy-done.4
  5.5 0.0 copy-start.5
  5.5 0.7 copy-done.5
  6.2 0.0 copy-start.6
  6.2 0.7 copy-done.6
  6.9 0.0 copy-start.7
  6.9 0.7 copy-done.7
  7.6 0.0 copy-start.8
  7.6 0.7 copy-done.8
  8.2 0.0 copy-start.9
  8.2 0.7 copy-done.9
  8.9 116.5 %shard_map.100 = bf16[64,2560]{1,0:T(8,128)(2,1)S(1)} custom-call(s32[32]{0:T(128)S(1)} %copy-done.7, s32[1,2]{1,0:T(1,128)S(1)} %copy-done.8, s32[1,2]{1,0:T(1,128)S(1)} %copy-done.9, bf16[64,2560]{1,0:T(8,128)(2,1)S(1)} %copy-done.3, bf16[64,2560]{1,0:T(8,128)(2,1)S(1)} %copy-done.4, bf16[80,2560]{1,0:T(8,128)(2,1)S(1)} %copy-done.1, ...), custom_call_target="tpu_custom_call" | custom-call | tf_op jit(solution)/shard_map/pallas_call | solution.py:589
  125.4 0.7 copy.12
Async XLA Ops:
  0.0 1.5 %copy-start = (bf16[128,7680]{1,0:T(8,128)(2,1)S(1)}, bf16[128,7680]{1,0:T(8,128)(2,1)}, u32[]{:S(2)}) copy-start(bf16[128,7680]{1,0:T(8,128)(2,1)} %proj_ref.1) | copy-start | bytes 5898244
  1.5 1.0 copy-start.1
  2.5 1.0 copy-start.2
  3.6 1.0 copy-start.3
  4.5 1.0 copy-start.4
  5.5 0.7 copy-start.5
  6.2 0.7 copy-start.6
  6.9 0.7 copy-start.7
  7.6 0.7 copy-start.8
  8.2 0.7 copy-start.9

commit v5 on v4

--- a/solution.py
+++ b/solution.py
@@ -523,35 +523,40 @@
         for slot in (2, 3, 1, 0):
             s = ranks[slot]
             span = pl.ds(pl.multiple_of(s * rows, rows), rows)
-            for h in range(heads):
-                lanes = slice(h * HEAD_DIM, (h + 1) * HEAD_DIM)
+            head_lanes = [slice(h * HEAD_DIM, (h + 1) * HEAD_DIM) for h in range(heads)]
+            nears, pasts = [], []
+            for lanes in head_lanes:
                 query = q_rows[span, lanes]
                 keys = ctx_k[pl.ds(s, LAGS), :, lanes].reshape(LAGS * rows, HEAD_DIM)
+                nears.append(lax.dot_general(
+                    query, k_rows[span, lanes], nt, preferred_element_type=jnp.float32
+                ))
+                pasts.append(lax.dot_general(
+                    query, keys, nt, preferred_element_type=jnp.float32
+                ))
+            near = jnp.concatenate(nears, axis=0) * HEAD_DIM ** (-0.5)
+            past = jnp.concatenate(pasts, axis=0) * HEAD_DIM ** (-0.5) + bias_all[s, 0:1, :]
+            highest = jnp.maximum(
+                jnp.max(near, axis=-1, keepdims=True), jnp.max(past, axis=-1, keepdims=True)
+            )
+            near = jnp.exp(near - highest)
+            past = jnp.exp(past - highest)
+            inverse = 1.0 / (
+                jnp.sum(near, axis=-1, keepdims=True) + jnp.sum(past, axis=-1, keepdims=True)
+            )
+            near = (near * inverse).astype(jnp.bfloat16)
+            past = (past * inverse).astype(jnp.bfloat16)
+            outs = []
+            for h, lanes in enumerate(head_lanes):
                 values = ctx_v[pl.ds(s, LAGS), :, lanes].reshape(LAGS * rows, HEAD_DIM)
                 own_values = buffer[
                     0, s, :, pl.ds(pl.multiple_of(rank * inner + h * HEAD_DIM, 128), HEAD_DIM)
                 ]
-                near = lax.dot_general(
-                    query, k_rows[span, lanes], nt, preferred_element_type=jnp.float32
-                ) * HEAD_DIM ** (-0.5)
-                past = lax.dot_general(
-                    query, keys, nt, preferred_element_type=jnp.float32
-                ) * HEAD_DIM ** (-0.5) + bias_all[s, 0:1, :]
-                highest = jnp.maximum(
-                    jnp.max(near, axis=-1, keepdims=True), jnp.max(past, axis=-1, keepdims=True)
-                )
-                near = jnp.exp(near - highest)
-                past = jnp.exp(past - highest)
-                inverse = 1.0 / (
-                    jnp.sum(near, axis=-1, keepdims=True) + jnp.sum(past, axis=-1, keepdims=True)
-                )
-                mixed = jnp.dot(
-                    (near * inverse).astype(jnp.bfloat16), own_values,
-                    preferred_element_type=jnp.float32,
-                ) + jnp.dot(
-                    (past * inverse).astype(jnp.bfloat16), values,
-                    preferred_element_type=jnp.float32,
-                )
+                block = slice(h * rows, (h + 1) * rows)
+                outs.append(jnp.dot(
+                    near[block], own_values, preferred_element_type=jnp.float32
+                ) + jnp.dot(past[block], values, preferred_element_type=jnp.float32))
+            for lanes, mixed in zip(head_lanes, outs):
                 mix_out[step, s, :, lanes] = mixed.astype(jnp.bfloat16)
             if slot:
                 copy = remote(mix_out.at[step, s], mix.at[step, rank], peers[slot])

time: 127 us -> 124 us (0.976)
  Pallas kernels: 116 us -> 114 us
    pallas_call x1, Pallas kernels: 116 us -> 114 us  [fused(): pl.pallas_call(functools.partial(fused_kernel, count), out_shape=jax.Shap...]
where the time goes in v5:
time: 124 us; the launch traced here: 123 us
  Pallas kernels  114 us (92%)
  local copies, waits for them, and re-layouts  9.59 us (8%)
    pallas_call x1, Pallas kernels, fused(): pl.pallas_call(functools.partial(fused_kernel, count), out_shape=jax.Shap...  114 us
    unnamed x21, local copies, waits for them, and re-layouts  9.59 us

profile of v5, /device:TPU:0, one launch (start us, length us, event | category | flops | bytes accessed | tf_op | source)
XLA Modules:
  0.0 123.3 jit_solution(6985890639704216856)
XLA Ops:
  0.0 0.0 copy-start
  0.0 1.5 %copy-done = bf16[128,7680]{1,0:T(8,128)(2,1)S(1)} copy-done((bf16[128,7680]{1,0:T(8,128)(2,1)S(1)}, bf16[128,7680]{1,0:T(8,128)(2,1)}, u32[]{:S(2)}) %copy-start) | copy-done | bytes 1966104
  1.5 0.0 copy-start.1
  1.5 1.0 copy-done.1
  2.5 0.0 copy-start.2
  2.6 1.0 copy-done.2
  3.6 0.0 copy-start.3
  3.6 1.0 copy-done.3
  4.5 0.0 copy-start.4
  4.5 1.0 copy-done.4
  5.5 0.0 copy-start.5
  5.5 0.7 copy-done.5
  6.2 0.0 copy-start.6
  6.2 0.7 copy-done.6
  6.9 0.0 copy-start.7
  6.9 0.7 copy-done.7
  7.6 0.0 copy-start.8
  7.6 0.7 copy-done.8
  8.2 0.0 copy-start.9
  8.2 0.7 copy-done.9
  8.9 113.7 %shard_map.100 = bf16[64,2560]{1,0:T(8,128)(2,1)S(1)} custom-call(s32[32]{0:T(128)S(1)} %copy-done.7, s32[1,2]{1,0:T(1,128)S(1)} %copy-done.8, s32[1,2]{1,0:T(1,128)S(1)} %copy-done.9, bf16[64,2560]{1,0:T(8,128)(2,1)S(1)} %copy-done.3, bf16[64,2560]{1,0:T(8,128)(2,1)S(1)} %copy-done.4, bf16[80,2560]{1,0:T(8,128)(2,1)S(1)} %copy-done.1, ...), custom_call_target="tpu_custom_call" | custom-call | tf_op jit(solution)/shard_map/pallas_call | solution.py:594
  122.6 0.7 copy.12
Async XLA Ops:
  0.0 1.5 %copy-start = (bf16[128,7680]{1,0:T(8,128)(2,1)S(1)}, bf16[128,7680]{1,0:T(8,128)(2,1)}, u32[]{:S(2)}) copy-start(bf16[128,7680]{1,0:T(8,128)(2,1)} %proj_ref.1) | copy-start | bytes 5898244
  1.5 1.0 copy-start.1
  2.5 1.0 copy-start.2
  3.6 1.0 copy-start.3
  4.5 1.0 copy-start.4
  5.5 0.7 copy-start.5
  6.2 0.7 copy-start.6
  6.9 0.7 copy-start.7
  7.6 0.7 copy-start.8
  8.2 0.7 copy-start.9
